TPU v7x, 32 devices: a whole 2x2x4 slice. The times are simulated.
32 devices in a mesh: lvl: 2 (over y), row: 16 (over z, x, core).
Axes of the slice: x: 2, y: 2, z: 4, core: 2. Of those that a mesh axis runs over, the one named last changes fastest.
Arguments:
- node_latent: float32 [8192, 512], P('row'), may hold values from -6 to 6
- edge_latent: float32 [81920, 512], P(('lvl', 'row')), may hold values from -6 to 6
- senders: int32 [81920], P(('lvl', 'row')), may hold values from 0 to 8191, as said below
- receivers: int32 [81920], P(('lvl', 'row')), may hold values from 0 to 8191, as said below
- live_edges: int32 [32], P(('lvl', 'row')), may hold values from 640 to 2560, as said below
- edge_w1: bfloat16 [2, 1536, 512], replicated, may hold values from -0.15625 to 0.15625
- edge_b1: float32 [2, 512], replicated, may hold values from -3 to 3
- edge_w2: bfloat16 [2, 512, 512], replicated, may hold values from -0.25 to 0.25
- edge_b2: float32 [2, 512], replicated, may hold values from -3 to 3
- edge_gain: float32 [2, 512], replicated, may hold values from 0.5 to 1.5
- edge_shift: float32 [2, 512], replicated, may hold values from -2 to 2
- node_w1: bfloat16 [2, 1024, 512], replicated, may hold values from -0.1875 to 0.1875
- node_b1: float32 [2, 512], replicated, may hold values from -3 to 3
- node_w2: bfloat16 [2, 512, 512], replicated, may hold values from -0.25 to 0.25
- node_b2: float32 [2, 512], replicated, may hold values from -3 to 3
- node_gain: float32 [2, 512], replicated, may hold values from 0.5 to 1.5
- node_shift: float32 [2, 512], replicated, may hold values from -2 to 2
- node_cotangent: float32 [8192, 512], P('row'), may hold values from -6 to 6
- edge_cotangent: float32 [81920, 512], P(('lvl', 'row')), may hold values from -6 to 6
Outputs:
- node_out: float32 [8192, 512], P('row')
- edge_out: float32 [81920, 512], P(('lvl', 'row'))
- node_grad: float32 [8192, 512], P('row')
- edge_grad: float32 [81920, 512], P(('lvl', 'row'))
- grad_edge_w1: float32 [2, 1536, 512], replicated
- grad_edge_b1: float32 [2, 512], replicated
- grad_edge_w2: float32 [2, 512, 512], replicated
- grad_edge_b2: float32 [2, 512], replicated
- grad_edge_gain: float32 [2, 512], replicated
- grad_edge_shift: float32 [2, 512], replicated
- grad_node_w1: float32 [2, 1024, 512], replicated
- grad_node_b1: float32 [2, 512], replicated
- grad_node_w2: float32 [2, 512, 512], replicated
- grad_node_b2: float32 [2, 512], replicated
- grad_node_gain: float32 [2, 512], replicated
- grad_node_shift: float32 [2, 512], replicated
- stream_rms: float32 [2, 4], replicated
Inputs may be any that keep to these rules, and one draw needn't show every extreme that they name: Edge block b (slots b * 2560 to (b + 1) * 2560 - 1) has receivers in node rows (b mod 16) * 512 to (b mod 16 + 1) * 512 - 1, never falling within the block, its first slot at the first of these rows and its last slot at the last; padded slots also carry such receivers. In each edge block, for each r, exactly 160 slots have senders in node rows r * 512 to (r + 1) * 512 - 1. `live_edges`: some edge block has all 2560 slots live in every draw.
All inputs are finite; a program needn't handle non-finite values.
Results may differ from a plain program's by a relative error of at most 0.02.
Values may be sent and summed in bfloat16 or wider, within the bound.
A program may use at most 320 MiB of HBM per device.

v0:
```python
import jax
import jax.numpy as jnp
from jax import lax
from jax.sharding import PartitionSpec as P

NORM_EPS = 1e-05


def contract(left, right, left_dim, right_dim):
    return lax.dot_general(
        left, right, (((left_dim,), (right_dim,)), ((), ())), preferred_element_type=jnp.float32
    )


def norm_rows(values, norm_gain, norm_shift):
    average = jnp.mean(values, axis=-1, keepdims=True)
    centered = values - average
    variance = jnp.mean(centered * centered, axis=-1, keepdims=True)
    return centered * lax.rsqrt(variance + NORM_EPS) * norm_gain + norm_shift


def mlp_forward(joined, first_w, first_b, second_w, second_b, norm_gain, norm_shift):
    pre_one = jnp.dot(joined, first_w, preferred_element_type=jnp.float32) + first_b
    active = jax.nn.silu(pre_one).astype(jnp.bfloat16)
    pre_two = jnp.dot(active, second_w, preferred_element_type=jnp.float32) + second_b
    return (norm_rows(pre_two, norm_gain, norm_shift), (joined, pre_one, active, pre_two))


def mlp_backward(saved, grad_out, first_w, second_w, norm_gain, norm_shift):
    joined, pre_one, active, pre_two = saved
    unused, pull_norm = jax.vjp(norm_rows, pre_two, norm_gain, norm_shift)
    d_two, d_gain, d_shift = pull_norm(grad_out)
    d_two = d_two.astype(jnp.bfloat16)
    d_second = contract(active, d_two, 0, 0)
    d_second_b = jnp.sum(d_two.astype(jnp.float32), axis=0)
    d_active = contract(d_two, second_w, 1, 1)
    unused_silu, pull_silu = jax.vjp(jax.nn.silu, pre_one)
    d_one = pull_silu(d_active)[0].astype(jnp.bfloat16)
    d_first = contract(joined, d_one, 0, 0)
    d_first_b = jnp.sum(d_one.astype(jnp.float32), axis=0)
    d_joined = contract(d_one, first_w, 1, 1)
    return (d_joined, (d_first, d_first_b, d_second, d_second_b, d_gain, d_shift))


def sender_picker(senders):

    def pick_rows(current, shard_rows, first_row):
        row_count = shard_rows.shape[0]
        inside = (senders >= 0) & (senders < row_count)
        fetched = jnp.take(shard_rows, jnp.clip(senders, 0, row_count - 1), axis=0)
        return jnp.where(inside[:, None], fetched, current)

    return pick_rows


def on_device(
    node_latent,
    edge_latent,
    senders,
    receivers,
    live_edges,
    edge_w1,
    edge_b1,
    edge_w2,
    edge_b2,
    edge_gain,
    edge_shift,
    node_w1,
    node_b1,
    node_w2,
    node_b2,
    node_gain,
    node_shift,
    node_cotangent,
    edge_cotangent,
):
    node_count = node_latent.shape[0]
    width = node_latent.shape[1]
    edge_count = edge_latent.shape[0]
    layer_total = edge_w1.shape[0]
    row_total = lax.axis_size("row")
    level_total = lax.axis_size("lvl")
    row_start = lax.axis_index("row") * node_count
    first_level = (lax.axis_index("lvl") == 0).astype(jnp.float32)
    live_mask = (jnp.arange(edge_count) < live_edges[0]).astype(jnp.float32)[:, None]
    recv_local = receivers - row_start
    onehot_low = (jnp.arange(node_count)[:, None] == recv_local[None, :]).astype(jnp.bfloat16)
    pick_rows = sender_picker(senders)
    node_state = node_latent
    edge_state = edge_latent
    saved_layers = []
    square_rows = []
    for layer_idx in range(layer_total):
        low_node = node_state.astype(jnp.bfloat16)
        low_edge = edge_state.astype(jnp.bfloat16)
        empty_rows = jnp.zeros((edge_count, width), jnp.bfloat16)
        gathered = pick_rows(
            empty_rows, lax.all_gather(low_node, "row", axis=0, tiled=True), jnp.int32(0)
        )
        joined_edge = jnp.concatenate(
            [low_edge, gathered, jnp.take(low_node, recv_local, axis=0)], axis=1
        )
        normed, edge_saved = mlp_forward(
            joined_edge,
            edge_w1[layer_idx],
            edge_b1[layer_idx],
            edge_w2[layer_idx],
            edge_b2[layer_idx],
            edge_gain[layer_idx],
            edge_shift[layer_idx],
        )
        update = normed * live_mask
        edge_state = edge_state + update
        partials = jnp.dot(
            onehot_low, update.astype(jnp.bfloat16), preferred_element_type=jnp.float32
        )
        received = lax.psum(partials, "lvl")
        joined_node = jnp.concatenate([low_node, received.astype(jnp.bfloat16)], axis=1)
        node_normed, node_saved = mlp_forward(
            joined_node,
            node_w1[layer_idx],
            node_b1[layer_idx],
            node_w2[layer_idx],
            node_b2[layer_idx],
            node_gain[layer_idx],
            node_shift[layer_idx],
        )
        node_state = node_state + node_normed
        saved_layers.append((edge_saved, node_saved))
        square_rows.append(
            jnp.stack(
                [
                    first_level * jnp.sum(node_state * node_state),
                    jnp.sum(edge_state * edge_state),
                    jnp.sum(update * update),
                    first_level * jnp.sum(node_normed * node_normed),
                ]
            )
        )
    squares = jnp.stack(square_rows)
    grad_edge = edge_cotangent
    grad_node = node_cotangent
    edge_list = []
    node_list = []
    for layer_idx in reversed(range(layer_total)):
        edge_saved, node_saved = saved_layers[layer_idx]
        d_joined, node_terms = mlp_backward(
            node_saved,
            grad_node,
            node_w1[layer_idx],
            node_w2[layer_idx],
            node_gain[layer_idx],
            node_shift[layer_idx],
        )
        grad_node = grad_node + d_joined[:, :width]
        d_received = d_joined[:, width:]
        d_update = grad_edge + jnp.take(d_received, recv_local, axis=0)
        d_edge_in, edge_terms = mlp_backward(
            edge_saved,
            d_update * live_mask,
            edge_w1[layer_idx],
            edge_w2[layer_idx],
            edge_gain[layer_idx],
            edge_shift[layer_idx],
        )
        grad_edge = grad_edge + d_edge_in[:, :width]
        d_send = d_edge_in[:, width : 2 * width]
        row_count = lax.axis_size("row") * node_count
        inside = (senders >= 0) & (senders < row_count)
        target = jnp.where(inside, senders, row_count)
        from_senders = lax.psum_scatter(
            jax.ops.segment_sum(d_send, target, num_segments=row_count + 1)[:row_count].astype(
                jnp.bfloat16
            ),
            "row",
            scatter_dimension=0,
            tiled=True,
        ).astype(jnp.float32)
        from_receivers = jax.ops.segment_sum(
            d_edge_in[:, 2 * width :], recv_local, num_segments=node_count, indices_are_sorted=True
        )
        local_terms = from_senders + from_receivers
        grad_node = grad_node + lax.psum(local_terms.astype(jnp.bfloat16), "lvl").astype(
            jnp.float32
        )
        edge_list.append(edge_terms)
        node_list.append(node_terms)
    edge_list = edge_list[::-1]
    node_list = node_list[::-1]
    edge_first = jnp.stack([layer_terms[0] for layer_terms in edge_list])
    edge_first_b = jnp.stack([layer_terms[1] for layer_terms in edge_list])
    edge_second = jnp.stack([layer_terms[2] for layer_terms in edge_list])
    edge_second_b = jnp.stack([layer_terms[3] for layer_terms in edge_list])
    edge_gains = jnp.stack([layer_terms[4] for layer_terms in edge_list])
    edge_shifts = jnp.stack([layer_terms[5] for layer_terms in edge_list])
    node_first = jnp.stack([layer_terms[0] for layer_terms in node_list])
    node_first_b = jnp.stack([layer_terms[1] for layer_terms in node_list])
    node_second = jnp.stack([layer_terms[2] for layer_terms in node_list])
    node_second_b = jnp.stack([layer_terms[3] for layer_terms in node_list])
    node_gains = jnp.stack([layer_terms[4] for layer_terms in node_list])
    node_shifts = jnp.stack([layer_terms[5] for layer_terms in node_list])
    edge_sums = lax.psum(
        (edge_first, edge_first_b, edge_second, edge_second_b, edge_gains, edge_shifts, squares),
        ("lvl", "row"),
    )
    node_sums = (
        lax.psum(node_first.astype(jnp.bfloat16), "row").astype(jnp.float32),
        lax.psum(node_first_b.astype(jnp.bfloat16), "row").astype(jnp.float32),
        lax.psum(node_second.astype(jnp.bfloat16), "row").astype(jnp.float32),
        lax.psum(node_second_b.astype(jnp.bfloat16), "row").astype(jnp.float32),
        lax.psum(node_gains.astype(jnp.bfloat16), "row").astype(jnp.float32),
        lax.psum(node_shifts.astype(jnp.bfloat16), "row").astype(jnp.float32),
    )
    node_entries = float(node_count * row_total * width)
    edge_entries = float(edge_count * row_total * level_total * width)
    entries = jnp.array([node_entries, edge_entries, edge_entries, node_entries], jnp.float32)
    stream_rms = jnp.sqrt(edge_sums[6] / entries[None, :])
    return (
        node_state,
        edge_state,
        grad_node,
        grad_edge,
        edge_sums[0],
        edge_sums[1],
        edge_sums[2],
        edge_sums[3],
        edge_sums[4],
        edge_sums[5],
        node_sums[0],
        node_sums[1],
        node_sums[2],
        node_sums[3],
        node_sums[4],
        node_sums[5],
        stream_rms,
    )


def solution(mesh):
    placed = (
        P("row", None),
        P(("lvl", "row"), None),
        P(("lvl", "row")),
        P(("lvl", "row")),
        P(("lvl", "row")),
        P(),
        P(),
        P(),
        P(),
        P(),
        P(),
        P(),
        P(),
        P(),
        P(),
        P(),
        P(),
        P("row", None),
        P(("lvl", "row"), None),
    )
    return jax.shard_map(
        on_device,
        mesh=mesh,
        in_specs=placed,
        out_specs=(
            P("row", None),
            P(("lvl", "row"), None),
            P("row", None),
            P(("lvl", "row"), None),
            P(),
            P(),
            P(),
            P(),
            P(),
            P(),
            P(),
            P(),
            P(),
            P(),
            P(),
            P(),
            P(),
        ),
        check_vma=False,
    )
```

profile of v0, /device:TPU:0, one launch (start us, length us, event | category | flops | bytes accessed | tf_op | source)
XLA Modules:
  0.0 1070.2 jit_solution(9156271400355171495)
XLA Ops:
  13.4 7.7 gather_fusion.1
  35.1 52.7 %all-gather.3.cloned.1.call-done = bf16[8192,512]{1,0:T(8,128)(2,1)} async-done(((bf16[512,512]{1,0:T(8,128)(2,1)}), bf16[8192,512]{1,0:T(8,128)(2,1)}) %all-gather.3.cloned.1.call-update) | async-done | bytes 8388624 | tf_op jit(solution)/shard_map/all_gather | solution.py:98
  87.8 12.2 %gather_fusion = bf16[2560,512]{1,0:T(8,128)(2,1)S(1)} fusion(bf16[8192,512]{1,0:T(8,128)(2,1)} %all-gather.3.cloned.1.call-done, s32[3072]{0:T(1024)S(1)} %pad_clamp_fusion.1), kind=kCustom, calls=%fused_computation.clone | custom fusion | bytes 5253120 | tf_op jit(solution)/shard_map/jit(_take)/gather | solution.py:50
  118.4 29.9 %all-reduce.18 = bf16[512,512]{1,0:T(8,128)(2,1)S(1)} all-reduce(f32[512,512]{1,0:T(8,128)S(1)} %fusion.19), channel_id=1, replica_groups=mesh['lvl'=2,'row'=16] {'lvl'}, use_global_device_ids=true, to_apply=%region_2.5 | all-reduce | flops 262144 | bytes 1572864 | tf_op jit(solution)/shard_map/psum | solution.py:117
  155.9 19.4 %copy.80 = f32[2560,512]{0,1:T(8,128)} copy(f32[2560,512]{1,0:T(8,128)} %param.44) | data formatting | bytes 10485760 | tf_op args[18]
  175.5 8.2 gather_fusion.3
  200.8 30.3 %all-gather.5.cloned.1.call-done = bf16[8192,512]{0,1:T(8,128)(2,1)} async-done(((bf16[512,512]{0,1:T(8,128)(2,1)}), bf16[8192,512]{0,1:T(8,128)(2,1)}) %all-gather.5.cloned.1.call-update) | async-done | bytes 8388624 | tf_op jit(solution)/shard_map/all_gather | solution.py:98
  231.1 11.4 %copy.71 = bf16[8192,512]{1,0:T(8,128)(2,1)} copy(bf16[8192,512]{0,1:T(8,128)(2,1)} %all-gather.5.cloned.1.call-done) | data formatting | bytes 16777216 | tf_op jit(solution)/shard_map/all_gather | solution.py:98
  242.5 12.8 %gather_fusion.2 = bf16[2560,512]{1,0:T(8,128)(2,1)} fusion(bf16[8192,512]{1,0:T(8,128)(2,1)} %copy.71, s32[3072]{0:T(1024)S(1)} %pad_clamp_fusion.1), kind=kCustom, calls=%fused_computation.3.clone | custom fusion | bytes 5253120 | tf_op jit(solution)/shard_map/jit(_take)/gather | solution.py:50
  277.4 30.6 %all-reduce.19 = bf16[512,512]{0,1:T(8,128)(2,1)S(1)} all-reduce(f32[512,512]{0,1:T(8,128)} %fusion.18), channel_id=1, replica_groups=mesh['lvl'=2,'row'=16] {'lvl'}, use_global_device_ids=true, to_apply=%region_7.10 | all-reduce | flops 262144 | bytes 1572864 | tf_op jit(solution)/shard_map/psum | solution.py:117
  317.5 7.9 gather_fusion.4
  331.5 7.5 fusion.106
  339.1 8.2 multiply_reduce_fusion.4
  353.6 7.8 fusion.26
  361.3 23.5 %scatter_custom_fusion = f32[8193,512]{1,0:T(8,128)} fusion(s32[2560]{0:T(1024)} %get-tuple-element.117, f32[]{:T(128)} %constant.93.clone.1, f32[2560,1536]{1,0:T(8,128)} %fusion.26), kind=kCustom, calls=%fused_computation.14 | custom fusion | flops 1310720 | bytes 22022656 | tf_op jit(solution)/shard_map/scatter-add | solution.py:172
  384.8 8.9 slice.257
  393.8 102.2 %reduce-scatter.3.cloned.1.call-done = bf16[512,512]{1,0:T(8,128)(2,1)} async-done(((bf16[8192,512]{1,0:T(8,128)(2,1)}), bf16[512,512]{1,0:T(8,128)(2,1)}) %reduce-scatter.3.cloned.1.call-update) | async-done | bytes 524304 | tf_op jit(solution)/shard_map/reduce_scatter | solution.py:171
  497.2 17.5 %scatter_custom_fusion.1 = f32[512,512]{1,0:T(8,128)S(1)} fusion(f32[512,512]{1,0:T(8,128)S(1)} %convert_element_type.154, s32[2560]{0:T(1024)S(1)} %get-tuple-element.108, f32[2560,1536]{1,0:T(8,128)} %fusion.26), kind=kCustom, calls=%fused_computation.32 | custom fusion | flops 1310720 | bytes 6291456 | tf_op jit(solution)/shard_map/scatter-add | solution.py:179
  528.9 15.4 %all-reduce.11.cloned.1.call-done = bf16[512,512]{0,1:T(8,128)(2,1)} async-done(((bf16[512,512]{0,1:T(8,128)(2,1)}), bf16[512,512]{0,1:T(8,128)(2,1)}) %all-reduce.11.cloned.1.call-update) | async-done | bytes 524304 | tf_op jit(solution)/shard_map/psum | solution.py:183
  550.3 7.6 gather_fusion.5
  564.0 10.8 %fusion.105 = (f32[512]{0:T(512)S(1)}, f32[2560]{0:T(1024)S(1)}, f32[2560,512]{0,1:T(8,128)S(1)}, f32[2560,512]{0,1:T(8,128)}) fusion(f32[512]{0:T(512)S(1)} %bitcast.140, f32[2560,512]{0,1:T(8,128)} %copy-done.2, f32[2560]{0:T(1024)S(1)} %copy-done.50, f32[2560]{0:T(1024)S(1)} %fusion.86, f32[2560,512]{0,1:T(8,128)} %copy.85, ...), kind=kLoop, calls=%fused_computation.226 | loop fusion | flops 11793408 | bytes 31494656 | tf_op jit(solution)/shard_map/transpose(jvp())/reduce_sum | solution.py:19
  586.0 8.0 fusion.29
  594.0 23.3 %scatter_custom_fusion.2 = f32[8193,512]{1,0:T(8,128)} fusion(s32[2560]{0:T(1024)} %get-tuple-element.117, f32[]{:T(128)} %constant.93.clone.1, f32[2560,1536]{1,0:T(8,128)} %fusion.29), kind=kCustom, calls=%fused_computation.12 | custom fusion | flops 1310720 | bytes 22022656 | tf_op jit(solution)/shard_map/scatter-add | solution.py:172
  617.3 8.9 slice.256
  637.0 8.6 convolution_bitcast_fusion
  656.3 8.1 convolution_bitcast_fusion.1
  664.4 66.7 %reduce-scatter.5.cloned.1.call-done = bf16[512,512]{1,0:T(8,128)(2,1)} async-done(((bf16[8192,512]{1,0:T(8,128)(2,1)}), bf16[512,512]{1,0:T(8,128)(2,1)}) %reduce-scatter.5.cloned.1.call-update) | async-done | bytes 524304 | tf_op jit(solution)/shard_map/reduce_scatter | solution.py:171
  732.3 17.7 %scatter_custom_fusion.3 = f32[512,512]{1,0:T(8,128)S(1)} fusion(f32[512,512]{1,0:T(8,128)S(1)} %convert_element_type.161, s32[2560]{0:T(1024)S(1)} %get-tuple-element.108, f32[2560,1536]{1,0:T(8,128)} %fusion.29), kind=kCustom, calls=%fused_computation.29 | custom fusion | flops 1310720 | bytes 6291456 | tf_op jit(solution)/shard_map/scatter-add | solution.py:179
  777.2 32.8 %all-reduce.2 = (bf16[2,512]{1,0:T(2,128)(2,1)S(1)}, bf16[2,512]{1,0:T(2,128)(2,1)S(1)}, bf16[2,512]{1,0:T(2,128)(2,1)S(1)}, bf16[2,512]{1,0:T(2,128)(2,1)S(1)}) all-reduce(bf16[2,512]{1,0:T(2,128)(2,1)S(1)} %pad_maximum_fusion.20, bf16[2,512]{1,0:T(2,128)(2,1)S(1)} %pad_maximum_fusion.21, ...), channel_id=1, replica_groups=mesh['lvl'=2,'row'=16] {'row'}, use_global_device_ids=true, to_apply=%region_43.47 | all-reduce | flops 4096 | bytes 16384 | tf_op jit(solution)/shard_map/psum | solution.py:208
  818.7 7.4 add.343
  833.6 37.3 %all-reduce = (f32[2,512]{1,0:T(2,128)}, f32[2,512]{1,0:T(2,128)}, f32[2,512]{1,0:T(2,128)}, f32[2,512]{1,0:T(2,128)}, f32[2,4]{1,0:T(2,128)S(1)}) all-reduce(f32[2,512]{1,0:T(2,128)S(1)} %pad_maximum_fusion.16, f32[2,512]{1,0:T(2,128)S(1)} %pad_maximum_fusion.17, ...), channel_id=1, replica_groups=mesh['lvl'=2,'row'=16] {'lvl','row'}, use_global_device_ids=true, to_apply=%region_29.33 | all-reduce | flops 4104 | bytes 32832 | tf_op jit(solution)/shard_map/psum | solution.py:202
  880.0 175.4 %all-reduce.15.cloned.1.call-done = (f32[2,1536,512]{2,1,0:T(8,128)}, f32[2,512,512]{2,1,0:T(8,128)}) async-done(((f32[2,1536,512]{2,1,0:T(8,128)}, f32[2,512,512]{2,1,0:T(8,128)}), (f32[2,1536,512]{2,1,0:T(8,128)}, f32[2,512,512]{2,1,0:T(8,128)})) %all-reduce.15.cloned.1.call-update) | async-done | bytes 8388624 | tf_op jit(solution)/shard_map/psum | solution.py:202
  (385 shorter events, 224.5 us)
Async XLA Ops:
  7.2 80.6 %all-gather.3.cloned.1.call-start = ((), (), s32[]{:S(2)}) async-start(), calls=%async_computation.2 | async-start | bytes 8912896 | tf_op jit(solution)/shard_map/all_gather | solution.py:98
  9.4 221.8 %all-gather.5.cloned.1.call-start = ((), (), s32[]{:S(2)}) async-start(), calls=%async_computation.3 | async-start | bytes 8912896 | tf_op jit(solution)/shard_map/all_gather | solution.py:98
  34.8 76.9 %copy-start.83 = (f32[1,512]{1,0:T(1,128)}, f32[1,512]{1,0:T(1,128)S(1)}, u32[]{:S(2)}) copy-start(f32[1,512]{1,0:T(1,128)S(1)} %get-tuple-element.128) | copy-start | bytes 6148
  34.9 153.3 %copy-start.57 = (f32[1,512]{1,0:T(1,128)}, f32[1,512]{1,0:T(1,128)S(1)}, u32[]{:S(2)}) copy-start(f32[1,512]{1,0:T(1,128)S(1)} %get-tuple-element.124) | copy-start | bytes 6148
  34.9 153.2 %copy-start.64 = (f32[1,512]{1,0:T(1,128)}, f32[1,512]{1,0:T(1,128)S(1)}, u32[]{:S(2)}) copy-start(f32[1,512]{1,0:T(1,128)S(1)} %get-tuple-element.126) | copy-start | bytes 6148
  35.0 118.5 %copy-start.59 = (f32[1,512]{1,0:T(1,128)}, f32[1,512]{1,0:T(1,128)S(1)}, u32[]{:S(2)}) copy-start(f32[1,512]{1,0:T(1,128)S(1)} %get-tuple-element.134) | copy-start | bytes 6148
  35.0 118.5 %copy-start.68 = (f32[1,512]{1,0:T(1,128)}, f32[1,512]{1,0:T(1,128)S(1)}, u32[]{:S(2)}) copy-start(f32[1,512]{1,0:T(1,128)S(1)} %get-tuple-element.136) | copy-start | bytes 6148
  114.0 74.2 %copy-start.49 = (f32[2560]{0:T(1024)}, f32[2560]{0:T(1024)S(1)}, u32[]{:S(2)}) copy-start(f32[2560]{0:T(1024)S(1)} %broadcast_multiply_fusion.1) | copy-start | bytes 30724
  114.6 73.5 %copy-start.51 = (f32[2560]{0:T(1024)}, f32[2560]{0:T(1024)S(1)}, u32[]{:S(2)}) copy-start(f32[2560]{0:T(1024)S(1)} %fusion.87) | copy-start | bytes 30724
  155.5 340.6 %reduce-scatter.3.cloned.1.call-start = ((), (), s32[]{:S(2)}) async-start(), calls=%async_computation.4 | async-start | bytes 8912896 | tf_op jit(solution)/shard_map/reduce_scatter | solution.py:171
  155.9 19.4 %copy-start.10 = (bf16[512,512]{0,1:T(8,128)(2,1)S(1)}, bf16[512,512]{0,1:T(8,128)(2,1)}, u32[]{:S(2)}) copy-start(bf16[512,512]{0,1:T(8,128)(2,1)} %convert_element_type.144) | copy-start | bytes 1572868
  325.4 13.6 %slice-start.2 = ((s8[5242880]{0:T(1024)(128)(4,1)}), s8[1048576]{0:T(1024)(128)(4,1)S(1)}, s32[]{:S(2)}) async-start(s8[5242880]{0:T(1024)(128)(4,1)} %bitcast.136), calls=%async_computation.12 | async-start | bytes 2097152
  331.5 18.6 %slice-start.6 = ((s8[5242880]{0:T(1024)(128)(4,1)}), s8[4194304]{0:T(1024)(128)(4,1)S(1)}, s32[]{:S(2)}) async-start(s8[5242880]{0:T(1024)(128)(4,1)} %bitcast.184), calls=%async_computation.16 | async-start | bytes 8388608
  339.0 11.0 %slice-start.7 = ((s8[5242880]{0:T(1024)(128)(4,1)}), s8[1048576]{0:T(1024)(128)(4,1)S(1)}, s32[]{:S(2)}) async-start(s8[5242880]{0:T(1024)(128)(4,1)} %bitcast.184), calls=%async_computation.17 | async-start | bytes 2097152
  393.8 150.5 %all-reduce.11.cloned.1.call-start = ((), (), s32[]{:S(2)}) async-start(), calls=%async_computation.5 | async-start | bytes 1048576 | tf_op jit(solution)/shard_map/psum | solution.py:183
  515.8 215.3 %reduce-scatter.5.cloned.1.call-start = ((), (), s32[]{:S(2)}) async-start(), calls=%async_computation.6 | async-start | bytes 8912896 | tf_op jit(solution)/shard_map/reduce_scatter | solution.py:171
  522.6 21.7 %copy-start.6 = (f32[512,512]{0,1:T(8,128)S(1)}, f32[512,512]{0,1:T(8,128)}, u32[]{:S(2)}) copy-start(f32[512,512]{0,1:T(8,128)} %copy-done.5) | copy-start | bytes 3145732
  522.6 21.7 %copy-start.16 = (f32[512,512]{0,1:T(8,128)S(1)}, f32[512,512]{0,1:T(8,128)}, u32[]{:S(2)}) copy-start(f32[512,512]{0,1:T(8,128)} %copy.94) | copy-start | bytes 3145732
  522.6 21.7 %copy-start.56 = (f32[512]{0:T(512)S(1)}, f32[512]{0:T(512)}, u32[]{:S(2)}) copy-start(f32[512]{0:T(512)} %copy-done.55) | copy-start | bytes 6148
  522.6 21.7 %copy-start.60 = (f32[1,512]{1,0:T(1,128)S(1)}, f32[1,512]{1,0:T(1,128)}, u32[]{:S(2)}) copy-start(f32[1,512]{1,0:T(1,128)} %copy-done.59) | copy-start | bytes 6148
  522.6 23.3 %copy-start.67 = (f32[512]{0:T(512)S(1)}, f32[512]{0:T(512)}, u32[]{:S(2)}) copy-start(f32[512]{0:T(512)} %copy-done.66) | copy-start | bytes 6148
  522.6 23.3 %copy-start.63 = (f32[512]{0:T(512)S(1)}, f32[512]{0:T(512)}, u32[]{:S(2)}) copy-start(f32[512]{0:T(512)} %copy-done.62) | copy-start | bytes 6148
  522.6 23.3 %copy-start.69 = (f32[1,512]{1,0:T(1,128)S(1)}, f32[1,512]{1,0:T(1,128)}, u32[]{:S(2)}) copy-start(f32[1,512]{1,0:T(1,128)} %copy-done.68) | copy-start | bytes 6148
  558.0 16.8 %slice-start = ((s8[5242880]{0:T(1024)(128)(4,1)}), s8[1048576]{0:T(1024)(128)(4,1)S(1)}, s32[]{:S(2)}) async-start(s8[5242880]{0:T(1024)(128)(4,1)} %bitcast.134), calls=%async_computation.10 | async-start | bytes 2097152
  563.9 10.8 %slice-start.1 = ((s8[5242880]{0:T(1024)(128)(4,1)}), s8[4194304]{0:T(1024)(128)(4,1)S(1)}, s32[]{:S(2)}) async-start(s8[5242880]{0:T(1024)(128)(4,1)} %bitcast.134), calls=%async_computation.11 | async-start | bytes 8388608
  563.9 10.8 %copy-start.52 = (f32[2560]{0:T(1024)S(1)}, f32[2560]{0:T(1024)}, u32[]{:S(2)}) copy-start(f32[2560]{0:T(1024)} %copy-done.51) | copy-start | bytes 30724
  564.0 10.8 %copy-start.65 = (f32[1,512]{1,0:T(1,128)S(1)}, f32[1,512]{1,0:T(1,128)}, u32[]{:S(2)}) copy-start(f32[1,512]{1,0:T(1,128)} %copy-done.64) | copy-start | bytes 6148
  626.3 245.2 %all-reduce.17.cloned.1.call-start = ((), (), s32[]{:S(2)}) async-start(), calls=%async_computation.9 | async-start | bytes 6291456 | tf_op jit(solution)/shard_map/psum | solution.py:207
  649.5 227.9 %all-reduce.13.cloned.1.call-start = ((), (), s32[]{:S(2)}) async-start(), calls=%async_computation.7 | async-start | bytes 1048576 | tf_op jit(solution)/shard_map/psum | solution.py:183
  751.0 304.4 %all-reduce.15.cloned.1.call-start = ((), (), s32[]{:S(2)}) async-start(), calls=%async_computation.8 | async-start | bytes 16777216 | tf_op jit(solution)/shard_map/psum | solution.py:202
  826.2 44.8 %copy-start.87 = (f32[4]{0:T(128)S(1)}, f32[4]{0:T(128)}, u32[]{:S(2)}) copy-start(f32[4]{0:T(128)} %constant.101) | copy-start | bytes 52
  832.1 45.3 %copy-start.8 = (f32[512,512]{0,1:T(8,128)S(1)}, f32[512,512]{0,1:T(8,128)}, u32[]{:S(2)}) copy-start(f32[512,512]{0,1:T(8,128)} %copy-done.7) | copy-start | bytes 3145732
  (91 other events, 363.6 us)
Sparse Core Ops, SparseCore 0:
  10.2 77.5 all-gather.2
  155.6 75.4 all-gather.4
  393.9 102.1 reduce-scatter.2
  515.9 28.3 all-reduce.10
  626.4 104.6 reduce-scatter.4
  735.7 103.6 all-reduce.16
  841.8 27.9 all-reduce.12
  876.3 179.1 all-reduce.14
where the time goes:
time: 1080 us; the launch traced here: 1070 us
  waiting for transfers between devices  443 us (41%)
  local copies, waits for them, and re-layouts  208 us (19%)
  other arithmetic  185 us (17%)
  blocking collectives  131 us (12%)
  matrix products  84.1 us (8%)
  between operations  18.9 us (2%)
    psum x1, waiting for transfers between devices, on_device(): lax.psum((edge_first, edge_first_b, edge_second, edge_second_b, edge_gain...  175 us
    reduce_scatter x2, waiting for transfers between devices, on_device(): lax.psum_scatter(jax.ops.segment_sum(d_send, target, num_segments=row_cou...  169 us
    all_gather x2, waiting for transfers between devices, on_device(): lax.all_gather(low_node, 'row', axis=0, tiled=True)  83.1 us
    unnamed x244, local copies, waits for them, and re-layouts  82.2 us
    psum x2, blocking collectives, on_device(): received = lax.psum(partials, 'lvl')  60.5 us
    dot_general x16, matrix products, contract(): lax.dot_general(left, right, (((left_dim,), (right_dim,)), ((), ())), pre...  56.8 us
    scatter-add x2, other arithmetic, on_device(): jax.ops.segment_sum(d_send, target, num_segments=row_count + 1)[:row_count]  46.8 us
    psum x1, blocking collectives, on_device(): lax.psum((edge_first, edge_first_b, edge_second, edge_second_b, edge_gain...  37.3 us
  transfers between devices with their start and end apart: 8, of which 6 were waited for; matrix products, arithmetic and copies ran while one was open for 18% of the time, Pallas kernels for 0%

commit v1 on v0

v1 whole, which is shorter than its diff:
```python
import functools

import jax
import jax.numpy as jnp
from jax import lax
from jax.experimental import pallas as pl
from jax.experimental.pallas import tpu as pltpu
from jax.sharding import PartitionSpec as P

MESH = pl.DeviceIdType.MESH
NORM_EPS = 1e-05
F32 = jnp.float32
BF16 = jnp.bfloat16
VMEM_BYTES = 61 * 2**20


NEAREST = ((0, 1, 2, 3), (1, 0, 2, 3), (2, 3, 1, 0), (3, 2, 1, 0))


class Grid:
    def __init__(self, levels, rows):
        self.L, self.R = levels, rows
        self.Z = 4
        self.X = rows // (2 * self.Z)
        self.l = lax.axis_index("lvl")
        row = lax.axis_index("row")
        self.row = row
        self.core = lax.rem(row, 2)
        self.x = lax.rem(row // 2, self.X)
        self.z = row // (2 * self.X)
        self.up = self.z < self.Z - 1
        self.down = self.z > 0

    def block(self, z, x, core):
        return (z * self.X + x) * 2 + core

    def mate(self):
        return (self.l, self.block(self.z, self.x, 1 - self.core))

    def at_z(self, z):
        return (self.l, self.block(jnp.clip(z, 0, self.Z - 1), self.x, self.core))

    def x_other(self, i):
        x = lax.rem(self.x + i, self.X)
        return x, (self.l, self.block(self.z, x, self.core))

    def l_other(self, i):
        l = lax.rem(self.l + i, self.L)
        return l, (l, self.row)

    def nth(self, k, z=None):
        z_here = self.z if z is None else z
        order = NEAREST
        out = jnp.int32(0)
        for z in range(4):
            for j in range(4):
                if order[z][j]:
                    out = jnp.where((z_here == z) & (k == j), order[z][j], out)
        return out

    def local(self, zk, z=None):
        return (zk // 2) == lax.rem(self.z if z is None else z, 2)

    def corner_z(self, q):
        side = lax.rem(lax.rem(self.z, 2) + q // 2, 2)
        return side * 2 + lax.rem(q, 2)

    def pair_z(self):
        return self.z + 1 - 2 * lax.rem(self.z, 2)

    def greet(self):
        barrier = pltpu.get_barrier_semaphore()

        def hello(who):
            pl.semaphore_signal(barrier, inc=1, device_id=who, device_id_type=MESH)

        hello(self.mate())
        for i in range(1, self.X):
            hello(self.x_other(i)[1])
        for i in range(1, self.L):
            hello(self.l_other(i)[1])
        pl.when(self.up)(lambda: hello(self.at_z(self.z + 1)))
        pl.when(self.down)(lambda: hello(self.at_z(self.z - 1)))
        pl.semaphore_wait(barrier, self.X + self.L - 1 + self.up.astype(jnp.int32) + self.down.astype(jnp.int32))


def only(when, act):
    if when is None:
        act()
    else:
        pl.when(when)(act)


def cuts(h):
    first = -(-h // 32) * 16
    return ((0, first), (first, h - first)) if h > first else ((0, h),)


class Gather:
    def __init__(self, grid, table, h, send_sem, recv_sem):
        self.g, self.table, self.h = grid, table, h
        self.cuts = cuts(h)
        self.send_sem, self.recv_sem = send_sem, recv_sem
        X, L = grid.X, grid.L
        self.per_column = X + L + 1
        self.per_sides = 2 * (X - 1) * (L - 1) + X - 1 + L - 1
        self.at_sides = 4 * self.per_column
        self.at_corners = self.at_sides + 4 * self.per_sides
        self.drain = False

    @staticmethod
    def sends(levels, rows):
        X, L = rows // 8, levels
        return 2 * (4 * (X + L + 1) + 4 * (2 * (X - 1) * (L - 1) + X + L - 2) + 8 * (X - 1) * (L - 1))

    def slot(self, block, l, s=None):
        start, size = (0, self.h) if s is None else self.cuts[s]
        return self.table.at[pl.ds(pl.multiple_of((block * self.g.L + l) * self.h + start, 16), size)]

    def push(self, at, block, l, s, who, when=None):
        place = self.slot(block, l, s)
        copy = pltpu.make_async_remote_copy(
            place, place, self.send_sem.at[2 * at + s], self.recv_sem.at[(block * self.g.L + l) * 2 + s], device_id=who, device_id_type=MESH
        )
        only(when, copy.wait_send if self.drain else copy.start)

    def arrived(self, block, l, s):
        if self.drain:
            return
        place = self.slot(block, l, s)
        pltpu.make_async_remote_copy(
            place, place, self.send_sem.at[0], self.recv_sem.at[(block * self.g.L + l) * 2 + s], device_id=self.g.mate(), device_id_type=MESH
        ).wait_recv()

    def column(self, k, s, own=False):
        g = self.g
        zk = g.nth(k)
        block = g.block(zk, g.x, g.core)
        at = k * self.per_column
        if not own:
            self.arrived(block, g.l, s)
        self.push(at, block, g.l, s, g.at_z(g.z + 1), g.up & (zk <= g.z))
        self.push(at + 1, block, g.l, s, g.at_z(g.z - 1), g.down & (zk >= g.z))
        for i in range(1, g.X):
            self.push(at + 1 + i, block, g.l, s, g.x_other(i)[1])
        for j in range(1, g.L):
            self.push(at + g.X + j, block, g.l, s, g.l_other(j)[1])
        self.push(at + g.X + g.L, block, g.l, s, g.mate())

    def sides(self, k, s):
        g = self.g
        zk = g.nth(k)
        even = lax.rem(zk, 2) == 0
        at = self.at_sides + k * self.per_sides
        for i in range(1, g.X):
            block = g.block(zk, g.x_other(i)[0], g.core)
            self.arrived(block, g.l, s)
            for j in range(1, g.L):
                self.push(at, block, g.l, s, g.l_other(j)[1], g.local(zk) & even)
                at = at + 1
            self.push(at, block, g.l, s, g.mate())
            at = at + 1
        for j in range(1, g.L):
            block = g.block(zk, g.x, g.core)
            l = g.l_other(j)[0]
            self.arrived(block, l, s)
            for i in range(1, g.X):
                self.push(at, block, l, s, g.x_other(i)[1], g.local(zk) & jnp.logical_not(even))
                at = at + 1
            self.push(at, block, l, s, g.mate())
            at = at + 1

    def corners(self, z, s, local):
        g = self.g
        q = lax.rem(z, 2) + (0 if local else 2)
        for i in range(1, g.X):
            block = g.block(z, lax.rem(g.x + i, g.X), g.core)
            for j in range(1, g.L):
                l = g.l_other(j)[0]
                at = self.at_corners + ((q * (g.X - 1) + i - 1) * (g.L - 1) + j - 1) * 2
                self.arrived(block, l, s)
                if local:
                    self.push(at, block, l, s, g.at_z(g.pair_z()))
                self.push(at + 1, block, l, s, g.mate())

    def mates(self, z, x):
        for l in range(self.g.L):
            for s in range(len(self.cuts)):
                self.arrived(self.g.block(z, x, 1 - self.g.core), l, s)

    def begin(self):
        for s in range(len(self.cuts)):
            self.column(0, s, own=True)

    def wave(self, k, s):
        g = self.g
        pl.when(k < 3)(lambda: self.column(k + 1, s))
        pl.when(k < 4)(lambda: self.sides(k, s))
        if g.L == 1:
            return
        two = len(self.cuts) == 2
        late = 1 - s if two else s
        back = 2 - s if two else 1
        for local, lag in ((True, back), (False, back + 1)):
            who = None if local else g.pair_z()
            kk = k - lag
            z = g.nth(jnp.clip(kk, 0, 3), who)
            pl.when((kk >= 0) & (kk < 4) & g.local(z, who))(lambda z=z, local=local: self.corners(z, late, local))

    def due(self, k, c):
        g = self.g
        own = c == 0
        far = c > g.X - 1
        off = jnp.where(own, 0, lax.rem(c - 1, max(g.X - 1, 1)) + 1)
        kk = jnp.where(own, k - 1, jnp.where(far, k - 3, k - 2))
        who = jnp.where(far, g.pair_z(), g.z)
        z = g.nth(jnp.clip(kk, 0, 3), who)
        there = (kk >= 0) & (kk < 4) & (own | g.local(z, who))
        return z, lax.rem(g.x + off, g.X), there

    def run(self, work=None):
        g = self.g
        parts = 2 * g.X - 1
        self.begin()

        def one(i, done):
            k, c = i // parts, lax.rem(i, parts)
            for s in range(len(self.cuts)):
                pl.when(c == s)(lambda s=s: self.wave(k, s))
            z, x, there = self.due(k, c)

            def ready():
                self.mates(z, x)
                if work is not None:
                    work(z, x, done)

            pl.when(there)(ready)
            return done + there.astype(jnp.int32)

        lax.fori_loop(0, 7 * parts, one, jnp.int32(0))

    def finish(self):
        self.drain = True
        self.begin()

        def one(k, carry):
            for s in range(len(self.cuts)):
                self.wave(k, s)
            return carry

        lax.fori_loop(0, 7, one, 0)


class Scatter:
    def __init__(self, grid, stage, inbox, h, send_sem, recv_sem):
        self.g, self.stage, self.inbox, self.h = grid, stage, inbox, h
        self.cuts = cuts(h)
        self.send_sem, self.recv_sem = send_sem, recv_sem
        X, L = grid.X, grid.L
        at = 0
        self.base = {}
        for name, count in self.parts(X, L):
            self.base[name] = at
            at += count
        at = 0
        self.out = {}
        for name, count in self.out_parts(X, L):
            self.out[name] = at
            at += count
        self.drain = False
        self.prepare()

    @staticmethod
    def parts(X, L):
        side = (X - 1) * (L - 1)
        return (("mate", 4 * X * L), ("pair", 2 * side), ("l2", side), ("x2", side), ("xc", 4 * (X - 1)), ("lc", 4 * (L - 1)), ("z", 5))

    @staticmethod
    def out_parts(X, L):
        side = (X - 1) * (L - 1)
        return (("mate", 4 * X * L), ("corner", 8 * side), ("xc", 4 * (X - 1)), ("lc", 4 * (L - 1)), ("z", 4))

    @staticmethod
    def receives(levels, rows):
        return sum(count for _, count in Scatter.parts(rows // 8, levels))

    @staticmethod
    def sends(levels, rows):
        return 2 * sum(count for _, count in Scatter.out_parts(rows // 8, levels))

    def slot(self, block, l, s=None):
        start, size = (0, self.h) if s is None else self.cuts[s]
        return self.stage.at[pl.ds(pl.multiple_of((block * self.g.L + l) * self.h + start, 16), size)]

    def push(self, out, block, l, s, at, who, when=None):
        start, size = self.cuts[s]
        copy = pltpu.make_async_remote_copy(
            self.slot(block, l, s),
            self.inbox.at[at, pl.ds(start, size)],
            self.send_sem.at[2 * out + s],
            self.recv_sem.at[2 * at + s],
            device_id=who,
            device_id_type=MESH,
        )
        only(when, copy.wait_send if self.drain else copy.start)

    def arrived(self, at, s):
        start, size = self.cuts[s]
        place = self.inbox.at[at, pl.ds(start, size)]
        pltpu.make_async_remote_copy(
            place, place, self.send_sem.at[0], self.recv_sem.at[2 * at + s], device_id=self.g.mate(), device_id_type=MESH
        ).wait_recv()

    def total(self, block, l, s, ats):
        start, size = self.cuts[s]
        for at in ats:
            self.arrived(at, s)
        out = self.slot(block, l, s)[...].astype(F32)
        for at in ats:
            out = out + self.inbox[at, start : start + size].astype(F32)
        return out

    def add(self, block, l, s, ats, when=None):
        if self.drain:
            return

        def act():
            self.slot(block, l, s)[...] = self.total(block, l, s, ats).astype(BF16)

        only(when, act)

    def each(self):
        return range(len(self.cuts))

    def to_mate(self, z, x):
        g = self.g
        for l in range(g.L):
            at = (z * g.X + x) * g.L + l
            for s in self.each():
                self.push(self.out["mate"] + at, g.block(z, x, 1 - g.core), l, s, self.base["mate"] + at, g.mate())

    def from_mate(self, z, x):
        g = self.g
        for l in range(g.L):
            for s in self.each():
                self.add(g.block(z, x, g.core), l, s, [self.base["mate"] + (z * g.X + x) * g.L + l])

    def corner_far(self, z, i):
        g = self.g
        block = g.block(z, lax.rem(g.x + i, g.X), g.core)
        for j in range(1, g.L):
            l = g.l_other(j)[0]
            spot = (lax.rem(z, 2) * (g.X - 1) + i - 1) * (g.L - 1) + j - 1
            for s in self.each():
                self.push(self.out["corner"] + spot, block, l, s, self.base["pair"] + spot, g.at_z(g.pair_z()))

    def corner_near(self, z, i):
        g = self.g
        x, x_dev = g.x_other(i)
        block = g.block(z, x, g.core)
        even = lax.rem(z, 2) == 0
        side = (g.X - 1) * (g.L - 1)
        for j in range(1, g.L):
            l, l_dev = g.l_other(j)
            spot = (lax.rem(z, 2) * (g.X - 1) + i - 1) * (g.L - 1) + j - 1
            out = self.out["corner"] + 2 * side + spot
            for s in self.each():
                self.add(block, l, s, [self.base["pair"] + spot])
                self.push(out, block, l, s, self.base["l2"] + (i - 1) * (g.L - 1) + g.L - j - 1, l_dev, even)
                self.push(out, block, l, s, self.base["x2"] + (g.X - i - 1) * (g.L - 1) + j - 1, x_dev, jnp.logical_not(even))

    def side_x(self, zk, i, waits):
        g = self.g
        x, x_dev = g.x_other(i)
        block = g.block(zk, x, g.core)
        ats = [self.base["l2"] + (i - 1) * (g.L - 1) + j - 1 for j in range(1, g.L)]
        for s in self.each():
            if ats and waits:
                self.add(block, g.l, s, ats)
            self.push(self.out["xc"] + zk * (g.X - 1) + i - 1, block, g.l, s, self.base["xc"] + zk * (g.X - 1) + g.X - i - 1, x_dev)

    def side_l(self, zk, waits):
        g = self.g
        block = g.block(zk, g.x, g.core)
        for j in range(1, g.L):
            l, l_dev = g.l_other(j)
            ats = [self.base["x2"] + (i - 1) * (g.L - 1) + j - 1 for i in range(1, g.X)]
            for s in self.each():
                if waits:
                    self.add(block, l, s, ats)
                self.push(self.out["lc"] + zk * (g.L - 1) + j - 1, block, l, s, self.base["lc"] + zk * (g.L - 1) + g.L - j - 1, l_dev)

    def around(self, zk):
        g = self.g
        ats = [self.base["xc"] + zk * (g.X - 1) + i - 1 for i in range(1, g.X)]
        return ats + [self.base["lc"] + zk * (g.L - 1) + j - 1 for j in range(1, g.L)]

    def column(self, zk):
        g = self.g
        block = g.block(zk, g.x, g.core)
        behind = jnp.where(zk > g.z, g.down, g.up)
        near = jnp.abs(zk - g.z) == 1
        spot = jnp.where(near & (zk < g.z), 4, zk)
        for s in self.each():
            self.add(block, g.l, s, self.around(zk))
            self.add(block, g.l, s, [self.base["z"] + zk], behind)
            self.push(self.out["z"] + zk, block, g.l, s, self.base["z"] + spot, g.at_z(jnp.where(zk > g.z, g.z + 1, g.z - 1)))

    def last(self, out):
        g = self.g
        for s in self.each():
            start, size = self.cuts[s]
            out[start : start + size, :] = self.total(g.row, g.l, s, self.around(g.z))
            for at, there in ((self.base["z"] + g.z, g.down), (self.base["z"] + 4, g.up)):

                def take(at=at, s=s, start=start, size=size):
                    self.arrived(at, s)
                    out[start : start + size, :] += self.inbox[at, start : start + size].astype(F32)

                pl.when(there)(take)

    @staticmethod
    def plan(X, hop=2):
        orders, spots = [], []
        for z in range(4):
            corners = (3, 2, 1, 0) if z < 2 else (0, 1, 2, 3)
            own = tuple(reversed(NEAREST[z]))
            order = []
            for j in range(4):
                order += [(corners[j], off) for off in range(1, X)] + [(own[j], 0)]
            orders.append(order)
            spots.append(({zk: max(m for m, (a, off) in enumerate(order) if a == zk and off) for zk in range(4)},
                          {zk: order.index((zk, 0)) for zk in range(4)}))
        names = ("far", "sx", "sl", "near", "sx_late", "sl_late", "column")
        due = [{name: {} for name in names} for _ in range(4)]

        def put(z, name, zk, step):
            while step in due[z][name]:
                step += 1
            due[z][name][step] = zk
            return step

        sides = [{}, {}, {}, {}]
        for z in range(4):
            pair = z + 1 - 2 * (z % 2)
            for zk in sorted(range(4), key=lambda a: spots[z][0][a]):
                near = zk // 2 == z % 2
                corner, own = spots[z][0][zk] + 1, spots[z][1][zk] + 1
                ready = put(z, "near", zk, max(corner, spots[pair][0][zk] + 1 + hop)) if near else put(z, "far", zk, corner)
                sx = put(z, "sx_late", zk, ready + hop) if near and zk % 2 == 0 else put(z, "sx", zk, corner)
                sl = put(z, "sl_late", zk, max(ready + hop, own)) if near and zk % 2 else put(z, "sl", zk, own)
                sides[z][zk] = max(sx, sl)
        for zk in range(4):
            for chain in (range(0, zk), range(3, zk, -1)):
                before = 0
                for z in chain:
                    before = put(z, "column", zk, max(sides[z][zk], before) + hop)
        steps = 1 + max(step for z in range(4) for name in names for step in due[z][name])
        return orders, due, steps

    def prepare(self):
        self.orders, self.due, self.steps = self.plan(self.g.X)
        self.blocks = 4 * self.g.X

    def pick(self, tables, m):
        out = jnp.int32(-1)
        for z in range(4):
            for at, value in tables[z].items():
                out = jnp.where((self.g.z == z) & (m == at), value, out)
        return out

    def place(self, m):
        g = self.g
        code = self.pick([{at: zk * g.X + off for at, (zk, off) in enumerate(order)} for order in self.orders], m)
        return code // g.X, lax.rem(g.x + lax.rem(code, g.X), g.X)

    def step(self, m):
        g = self.g

        def first():
            self.to_mate(*self.place(m))

        def second():
            self.from_mate(*self.place(m - 1))

        pl.when(m < self.blocks)(first)
        pl.when((m >= 1) & (m <= self.blocks))(second)

        def send(name, act, over_x):
            zk = self.pick([due[name] for due in self.due], m)

            def go():
                if over_x:
                    for i in range(1, g.X):
                        act(zk, i)
                else:
                    act(zk)

            pl.when(zk >= 0)(go)

        send("column", self.column, False)
        send("sl_late", lambda zk: self.side_l(zk, True), False)
        send("sx_late", lambda zk, i: self.side_x(zk, i, True), True)
        if g.L > 1:
            send("near", self.corner_near, True)
            send("far", self.corner_far, True)
        send("sl", lambda zk: self.side_l(zk, False), False)
        send("sx", lambda zk, i: self.side_x(zk, i, False), True)

    def run(self, work=None, ahead=4):
        def one(m, carry):
            if work is not None:
                work(m)
            self.step(m)

            def wait():
                self.drain = True
                self.step(m - ahead)
                self.drain = False

            pl.when(m >= ahead)(wait)
            return carry

        lax.fori_loop(0, self.steps, one, 0)
        self.ahead = ahead

    def finish(self):
        self.drain = True

        def one(m, carry):
            self.step(m)
            return carry

        lax.fori_loop(self.steps - self.ahead, self.steps, one, 0)


def dot(left, right):
    return jnp.dot(left, right, preferred_element_type=F32)


def dot_nt(left, right):
    return lax.dot_general(left, right, (((1,), (1,)), ((), ())), preferred_element_type=F32)


def dot_tn(left, right):
    return lax.dot_general(left, right, (((0,), (0,)), ((), ())), preferred_element_type=F32)


def fold(values):
    rows, width = values.shape
    return jnp.sum(values.reshape(rows // 8, 8, width), axis=0)


def norm_parts(values):
    average = jnp.mean(values, axis=-1, keepdims=True)
    centered = values - average
    scale = lax.rsqrt(jnp.mean(centered * centered, axis=-1, keepdims=True) + NORM_EPS)
    return centered * scale, scale


def norm_back(normed, scale, d_normed):
    mean_d = jnp.mean(d_normed, axis=-1, keepdims=True)
    mean_dn = jnp.mean(d_normed * normed, axis=-1, keepdims=True)
    return scale * (d_normed - mean_d - normed * mean_dn)


def silu_back(pre, d_active):
    gate = lax.logistic(pre)
    return d_active * (gate * (1.0 + pre * (1.0 - gate)))


def order_kernel(row_total, node_count, senders, receivers, live, edges, cot, cols_out, rows_out, edges_out, cot_out, place, side, joined):
    tiles = senders.shape[0]
    count = tiles * 128
    group = count // row_total
    width = edges.shape[1]
    first = lax.axis_index("row") * node_count
    lane = lax.broadcasted_iota(jnp.int32, (128, 128), 1)
    sub = lax.broadcasted_iota(jnp.int32, (128, 128), 0)
    before = (sub < lane).astype(BF16)
    owner_ids = lax.broadcasted_iota(jnp.int32, (row_total, 128), 0)
    carry = owner_ids[:, :1].astype(F32) * group
    for tile in range(tiles):
        send = senders[tile : tile + 1, :]
        recv = receivers[tile : tile + 1, :] - first
        owner = lax.div(send, node_count)
        local = send - owner * node_count
        mine = owner_ids == owner
        ranks = dot(mine.astype(BF16), before) + carry
        spot = jnp.sum(jnp.where(mine, ranks, 0.0), axis=0, keepdims=True)
        carry = carry + jnp.sum(mine.astype(F32), axis=1, keepdims=True)
        place[tile : tile + 1, :] = spot.astype(jnp.int32)
        alive = (lane[:1] + tile * 128 < live[0, 0]).astype(jnp.int32)
        facts = jnp.where(sub == 0, lax.div(local, 16), 0)
        facts = jnp.where(sub == 1, lax.rem(local, 16), facts)
        facts = jnp.where(sub == 2, lax.div(recv, 16), facts)
        facts = jnp.where(sub == 3, lax.rem(recv, 16), facts)
        facts = jnp.where(sub == 4, alive, facts).astype(F32)
        side[:, pl.ds(tile * 128, 128)] = facts[:16].astype(BF16)
        joined[pl.ds(tile * 128, 128), pl.ds(2 * width, 128)] = facts.T.astype(BF16)
        joined[pl.ds(tile * 128, 128), pl.ds(0, width)] = edges[pl.ds(tile * 128, 128), :].astype(BF16)
        joined[pl.ds(tile * 128, 128), pl.ds(width, width)] = cot[pl.ds(tile * 128, 128), :].astype(BF16)

    def one(pair, carry):
        start = pl.multiple_of(pair * 2 * group, 2 * group)
        ids = lax.broadcasted_iota(jnp.int32, (2 * group, 128), 0) + start
        pick = jnp.concatenate([(ids == place[tile : tile + 1, :]).astype(BF16) for tile in range(tiles)], axis=1)
        moved = dot(pick, joined[...])
        edges_out[pl.ds(start, 2 * group), :] = moved[:, :width].astype(BF16)
        cot_out[pl.ds(start, 2 * group), :] = moved[:, width : 2 * width].astype(BF16)
        cols = moved[:, 2 * width :]
        lanes = lax.broadcasted_iota(jnp.int32, cols.shape, 1)
        sent = cols[:, 0:1] * 16.0 + cols[:, 1:2]
        got = cols[:, 2:3] * 16.0 + cols[:, 3:4]
        cols_out[pl.ds(start, 2 * group), :] = jnp.where(lanes == 0, sent, jnp.where(lanes == 1, got, jnp.where(lanes == 2, cols[:, 4:5], 0.0)))
        for half in range(2):
            rows = dot_nt(side[...], pick[half * group : (half + 1) * group])
            rows_out[pair * 2 + half] = jnp.concatenate(
                [rows[0:1] * 16.0 + rows[1:2], rows[2:3] * 16.0 + rows[3:4], rows[4:10]], axis=0
            )
        return carry

    lax.fori_loop(0, row_total // 2, one, 0)


def order_edges(node_count, senders, receivers, live, edges, cot):
    row_total = lax.axis_size("row")
    count, width = edges.shape
    tiles = count // 128
    vmem = pl.BlockSpec(memory_space=pltpu.VMEM)
    return pl.pallas_call(
        functools.partial(order_kernel, row_total, node_count),
        out_shape=(
            jax.ShapeDtypeStruct((count, 128), F32),
            jax.ShapeDtypeStruct((row_total, 8, count // row_total), F32),
            jax.ShapeDtypeStruct((count, width), BF16),
            jax.ShapeDtypeStruct((count, width), BF16),
            jax.ShapeDtypeStruct((tiles, 128), jnp.int32),
        ),
        in_specs=[vmem, vmem, pl.BlockSpec(memory_space=pltpu.SMEM), vmem, vmem],
        out_specs=(vmem,) * 5,
        scratch_shapes=[pltpu.VMEM((16, count), BF16), pltpu.VMEM((count, 2 * width + 128), BF16)],
        compiler_params=pltpu.CompilerParams(vmem_limit_bytes=VMEM_BYTES),
        name="order_edges",
    )(senders.reshape(tiles, 128), receivers.reshape(tiles, 128), live.reshape(1, 1), edges, cot)


def restore_kernel(place, update, d_edge, edges, cot, edge_out, cot_out):
    tiles = place.shape[0]
    count, width = update.shape
    parts = edges.shape[0] // 128
    lane = lax.broadcasted_iota(jnp.int32, (128, 128), 1).astype(F32)
    pick = []
    for part in range(parts):
        spot = jnp.broadcast_to(place[pl.ds(pl.program_id(0) * parts + part, 1), :], (128, 128)).astype(F32).T
        pick.append(jnp.concatenate([(spot == lane + float(128 * j)).astype(BF16) for j in range(tiles)], axis=1))
    pick = jnp.concatenate(pick, axis=0)
    edge_out[...] = edges[...] + dot(pick, update[...])
    cot_out[...] = cot[...] + dot(pick, d_edge[...])


def restore_edges(place, update, d_edge, edges, cot):
    count, width = edges.shape
    whole = lambda shape: pl.BlockSpec(shape, lambda i: (0, 0))
    size = 512 if count % 512 == 0 else 128
    part = pl.BlockSpec((size, width), lambda i: (i, 0))
    return pl.pallas_call(
        restore_kernel,
        grid=(count // size,),
        out_shape=(jax.ShapeDtypeStruct((count, width), F32),) * 2,
        in_specs=[whole(place.shape), whole(update.shape), whole(d_edge.shape), part, part],
        out_specs=(part, part),
        compiler_params=pltpu.CompilerParams(vmem_limit_bytes=VMEM_BYTES),
        name="restore_edges",
    )(place, update, d_edge, edges, cot)


def one_hot_cols(ids, count):
    lanes = lax.broadcasted_iota(jnp.int32, (ids.shape[0], count), 1).astype(F32)
    return (ids == lanes).astype(BF16)


def one_hot_rows(ids, count):
    subs = lax.broadcasted_iota(jnp.int32, (count, ids.shape[1]), 0).astype(F32)
    return (ids == subs).astype(BF16)


def load_all(pairs, sems):
    copies = [pltpu.make_async_copy(src, dst, sems.at[i]) for i, (src, dst) in enumerate(pairs)]
    for copy in copies:
        copy.start()
    return copies


def forward_kernel(
    layer, levels, rows, first_layer,
    node, edges, before, cols, rows_of, b1, b2, gain, shift, nb1, nb2, ngain, nshift, w1_all, w2_all, nw1_all, nw2_all,
    sent_out, pre_out, normed_out, update_out, edges_out, scale_out, block_out, node_out, recv_out, npre_out, nnormed_out, nscale_out, tally,
    table, total, cast, near, far, w1, w2, nw1, nw2, out_buf, scale_buf,
    load_sem, out_sem, send_sem, recv_sem, near_send, near_recv,
):
    g = Grid(levels, rows)
    h = node.shape[0]
    count, width = edges.shape
    group = count // rows
    node_count = h * levels
    loads = load_all(((w1_all.at[layer], w1), (w2_all.at[layer], w2), (nw1_all.at[layer], nw1), (nw2_all.at[layer], nw2)), load_sem)
    ag = Gather(g, table, h, send_sem, recv_sem)
    ag.slot(g.row, g.l)[...] = node[...].astype(BF16)
    tally[...] = jnp.zeros_like(tally)
    total[...] = jnp.zeros_like(total)
    g.greet()
    wide = lambda ref: ref[layer : layer + 1, :]
    outs = (sent_out, pre_out, normed_out, update_out) + ((edges_out,) if first_layer else ())

    def leave(n, place):
        slot = lax.rem(n, 2)
        copies = [pltpu.make_async_copy(out_buf.at[slot, i], ref.at[place], out_sem.at[slot, i]) for i, ref in enumerate(outs)]
        return copies + [pltpu.make_async_copy(scale_buf.at[slot], scale_out.at[place], out_sem.at[slot, 5])]

    def work(z, x, n):
        def own():
            for copy in loads:
                copy.wait()
            here = table[pl.ds(pl.multiple_of(g.row * node_count, 16), node_count), :]
            cast[...] = dot(here, w1[2 * width :, :]).astype(BF16)
            block_out[...] = here

        pl.when(n == 0)(own)
        pair = g.block(z, x, 0)
        place = pl.ds(pl.multiple_of(pair * group, 2 * group), 2 * group)

        def free():
            for copy in leave(n, place):
                copy.wait()

        pl.when(n >= 2)(free)
        slot = lax.rem(n, 2)
        cols_here = cols[place, :]
        send_pick = one_hot_cols(cols_here[:, 0:1], node_count)
        recv_pick = one_hot_cols(cols_here[:, 1:2], node_count)
        start = pl.multiple_of(pair * node_count, 16)
        sent = jnp.concatenate(
            [
                dot(send_pick[:group], table[pl.ds(start, node_count), :]).astype(BF16),
                dot(send_pick[group:], table[pl.ds(start + node_count, node_count), :]).astype(BF16),
            ],
            axis=0,
        )
        out_buf[slot, 0] = sent
        pre = dot(edges[place, :], w1[:width, :]) + dot(sent, w1[width : 2 * width, :]) + dot(recv_pick, cast[...]) + wide(b1)
        out_buf[slot, 1] = pre.astype(BF16)
        active = (pre * lax.logistic(pre)).astype(BF16)
        normed, scale = norm_parts(dot(active, w2[...]) + wide(b2))
        out_buf[slot, 2] = normed.astype(BF16)
        scale_buf[slot] = jnp.broadcast_to(scale, (2 * group, 128))
        update = (normed * wide(gain) + wide(shift)) * cols_here[:, 2:3]
        update_low = update.astype(BF16)
        edge = edges[place, :].astype(F32) + update
        if first_layer:
            out_buf[slot, 3] = update_low
            out_buf[slot, 4] = edge.astype(BF16)
        else:
            out_buf[slot, 3] = (before[place, :].astype(F32) + update).astype(BF16)
        tally[8:16, :] += fold(edge * edge)
        tally[16:24, :] += fold(update * update)
        for half in range(2):
            pick = one_hot_rows(rows_of[pair + half][1:2, :], node_count)
            total[...] += dot(pick, update_low[half * group : (half + 1) * group])
        for copy in leave(n, place):
            copy.start()

    ag.run(work)
    copies = []
    for j in range(1, levels):
        l, l_dev = g.l_other(j)
        near[j - 1] = total[pl.ds(pl.multiple_of(l * h, h), h), :].astype(BF16)
        copy = pltpu.make_async_remote_copy(
            near.at[j - 1], far.at[levels - 1 - j], near_send.at[j - 1], near_recv.at[levels - 1 - j], device_id=l_dev, device_id_type=MESH
        )
        copy.start()
        copies.append(copy)
    received = total[pl.ds(pl.multiple_of(g.l * h, h), h), :]
    npre = dot(node[...].astype(BF16), nw1[:width, :]) + wide(nb1)
    for copy in copies:
        copy.wait()
    for j in range(1, levels):
        received = received + far[j - 1].astype(F32)
    received = received.astype(BF16)
    recv_out[...] = received
    npre = npre + dot(received, nw1[width:, :])
    npre_out[...] = npre
    nnormed, nscale = norm_parts(dot((npre * lax.logistic(npre)).astype(BF16), nw2[...]) + wide(nb2))
    nnormed_out[...] = nnormed
    nscale_out[...] = jnp.broadcast_to(nscale, (h, 128))
    change = nnormed * wide(ngain) + wide(nshift)
    new = node[...] + change
    node_out[...] = new
    tally[0:8, :] = fold(new * new)
    tally[24:32, :] = fold(change * change)
    for n in range(2):
        for copy in leave(n, pl.ds(0, 2 * group)):
            copy.wait()
    ag.finish()


def forward_layer(layer, node, edges, before, cols, rows_of, small, weights):
    levels, rows = lax.axis_size("lvl"), lax.axis_size("row")
    h, width = node.shape
    count = edges.shape[0]
    group = count // rows
    vmem = pl.BlockSpec(memory_space=pltpu.VMEM)
    hbm = pl.BlockSpec(memory_space=pl.ANY)
    first_layer = layer == 0
    shape = jax.ShapeDtypeStruct
    outs = (
        shape((count, width), BF16),
        shape((count, width), BF16),
        shape((count, width), BF16),
        shape((count, width), BF16),
        shape((count, width) if first_layer else (16, 128), BF16),
        shape((count, 128), F32),
        shape((h * levels, width), BF16),
        shape((h, width), F32),
        shape((h, width), BF16),
        shape((h, width), F32),
        shape((h, width), F32),
        shape((h, 128), F32),
        shape((32, width), F32),
    )
    ins = (node, edges, before, cols, rows_of) + small + weights
    others = max(levels - 1, 1)
    return pl.pallas_call(
        functools.partial(forward_kernel, layer, levels, rows, first_layer),
        out_shape=outs,
        in_specs=[vmem] * (len(ins) - 4) + [hbm] * 4,
        out_specs=(hbm,) * 6 + (vmem,) * (len(outs) - 6),
        scratch_shapes=[
            pltpu.VMEM((rows * h * levels, width), BF16),
            pltpu.VMEM((h * levels, width), F32),
            pltpu.VMEM((h * levels, width), BF16),
            pltpu.VMEM((others, h, width), BF16),
            pltpu.VMEM((others, h, width), BF16),
        ]
        + [pltpu.VMEM(weight.shape[1:], BF16) for weight in weights]
        + [
            pltpu.VMEM((2, 5, 2 * group, width), BF16),
            pltpu.VMEM((2, 2 * group, 128), F32),
            pltpu.SemaphoreType.DMA((4,)),
            pltpu.SemaphoreType.DMA((2, 6)),
            pltpu.SemaphoreType.DMA((Gather.sends(levels, rows),)),
            pltpu.SemaphoreType.DMA((2 * rows * levels,)),
            pltpu.SemaphoreType.DMA((others,)),
            pltpu.SemaphoreType.DMA((others,)),
        ],
        compiler_params=pltpu.CompilerParams(collective_id=1 + layer, has_side_effects=True, vmem_limit_bytes=VMEM_BYTES),
        name=f"forward_{layer}",
    )(*ins)


def backward_kernel(
    layer, levels, rows, last_layer,
    d_node, block, recv, npre, nnormed, nscale, cols, rows_of, scale, gain, ngain, d_before, d_edges, pre, normed, edges, sent, w1_all, w2_all, nw1_all, nw2_all,
    d_node_out, d_edges_out, d_change_out, grads, tally,
    stage, inbox, bufs, d_recv, turned, own_sum, out_buf, w1, w2, nw1, nw2,
    load_sem, out_sem, send_sem, recv_sem, near_send, near_recv,
):
    g = Grid(levels, rows)
    h, width = d_node.shape
    count = pre.shape[0]
    group = count // rows
    node_count = h * levels
    loads = load_all(
        ((nw2_all.at[layer], nw2), (nw1_all.at[layer], nw1), (w1_all.at[layer], w1), (w2_all.at[layer], w2))
        + tuple((src, bufs.at[i]) for i, src in enumerate((d_edges, pre, normed, edges, sent))),
        load_sem,
    )
    rs = Scatter(g, stage, inbox, h, send_sem, recv_sem)
    wide = lambda ref: ref[layer : layer + 1, :]
    mine = pl.ds(pl.multiple_of(g.l * h, h), h)
    own_sum[...] = jnp.zeros_like(own_sum)
    tally[...] = jnp.zeros_like(tally)
    for copy in loads[:2]:
        copy.wait()
    tally[48:56, :] = fold(d_node[...] * nnormed[...])
    tally[56:64, :] = fold(d_node[...])
    d_two = norm_back(nnormed[...], nscale[:, 0:1], d_node[...] * wide(ngain)).astype(BF16)
    tally[40:48, :] = fold(d_two.astype(F32))
    d_one = silu_back(npre[...], dot_nt(d_two, nw2[...])).astype(BF16)
    tally[32:40, :] = fold(d_one.astype(F32))
    d_recv[mine, :] = dot_nt(d_one, nw1[width:, :]).astype(BF16)
    g.greet()
    copies = []
    for j in range(1, levels):
        copy = pltpu.make_async_remote_copy(
            d_recv.at[mine], d_recv.at[mine], near_send.at[j - 1], near_recv.at[levels - 1 - j], device_id=g.l_other(j)[1], device_id_type=MESH
        )
        copy.start()
        copies.append(copy)
    d_node_out[...] = d_node[...] + dot_nt(d_one, nw1[:width, :])
    active = (npre[...] * lax.logistic(npre[...])).astype(BF16)
    grads[4 * width + width : 6 * width, :] = dot_tn(recv[...], d_one).astype(BF16)
    grads[4 * width : 5 * width, :] = dot_tn(block[mine, :], d_one).astype(BF16)
    grads[6 * width : 7 * width, :] = dot_tn(active, d_two).astype(BF16)
    for copy in copies:
        copy.wait()
    for copy in loads[2:]:
        copy.wait()

    def work(i):
        z, x = rs.place(i)
        pair = g.block(z, x, 0)
        start = pl.multiple_of(pair * group, 2 * group)
        place = pl.ds(start, 2 * group)
        if not last_layer:
            earlier = pltpu.make_async_copy(d_before.at[place], out_buf.at[lax.rem(i, 2), 0], out_sem.at[lax.rem(i, 2), 0])
            earlier.start()
        cols_here = cols[place, :]
        recv_pick = one_hot_cols(cols_here[:, 1:2], node_count)
        d_edge = bufs[0, place, :].astype(F32)
        d_update = (d_edge + dot(recv_pick, d_recv[...])) * cols_here[:, 2:3]
        norm_here = bufs[2, place, :].astype(F32)
        tally[16:24, :] += fold(d_update * norm_here)
        tally[24:32, :] += fold(d_update)
        d_two = norm_back(norm_here, scale[place, 0:1], d_update * wide(gain)).astype(BF16)
        tally[8:16, :] += fold(d_two.astype(F32))
        pre_here = bufs[1, place, :].astype(F32)
        gate = lax.logistic(pre_here)
        d_one = (dot_nt(d_two, w2[...]) * (gate * (1.0 + pre_here * (1.0 - gate)))).astype(BF16)
        tally[0:8, :] += fold(d_one.astype(F32))
        bufs[0, place, :] = d_one
        bufs[1, place, :] = (pre_here * gate).astype(BF16)
        bufs[2, place, :] = d_two
        d_here = dot_nt(d_one, w1[:width, :])
        slot = lax.rem(i, 2)
        used = [
            pltpu.make_async_copy(out_buf.at[slot, n], ref.at[place], out_sem.at[slot, n])
            for n, ref in enumerate((d_edges_out, d_change_out))
            if n or last_layer
        ]

        def free():
            for copy in used:
                copy.wait()

        pl.when(i >= 2)(free)
        if last_layer:
            out_buf[slot, 0] = (d_edge + d_here).astype(BF16)
            out_buf[slot, 1] = d_here.astype(BF16)
        else:
            earlier.wait()
            out_buf[slot, 1] = (out_buf[slot, 0].astype(F32) + d_here).astype(BF16)
        for copy in used:
            copy.start()
        d_sent = dot_nt(d_one, w1[width : 2 * width, :]).astype(BF16)
        for half in range(2):
            ids = rows_of[pair + half]
            part = slice(half * group, (half + 1) * group)
            own_sum[...] += dot(one_hot_rows(ids[1:2, :], node_count), d_one[part])
            spot = pl.ds(pl.multiple_of((pair + half) * node_count, 16), node_count)
            stage[spot, :] = dot(one_hot_rows(ids[0:1, :], node_count), d_sent[part]).astype(BF16)

        def close():
            low = own_sum[...].astype(BF16)
            spot = pl.ds(pl.multiple_of(g.row * node_count, 16), node_count)
            stage[spot, :] = (stage[spot, :].astype(F32) + dot_nt(low, w1[2 * width :, :])).astype(BF16)
            grads[2 * width : 3 * width, :] = dot_tn(block[...], low).astype(BF16)

        pl.when(i == rs.blocks - 1)(close)

    def step(m):
        pl.when(m < rs.blocks)(lambda: work(m))
        for n, (at, left, right) in enumerate(((0, 3, 0), (1, 4, 0), (3, 1, 2))):

            def grad(at=at, left=left, right=right):
                grads[at * width : (at + 1) * width, :] = dot_tn(bufs[left], bufs[right]).astype(BF16)

            pl.when(m == rs.blocks + n)(grad)

    rs.run(step)
    rs.last(turned)
    d_node_out[...] += turned[...]
    for slot in range(2):
        for n, ref in enumerate((d_edges_out, d_change_out)):
            if n or last_layer:
                pltpu.make_async_copy(out_buf.at[slot, n], ref.at[pl.ds(0, 2 * group)], out_sem.at[slot, n]).wait()
    rs.finish()


def backward_layer(layer, last_layer, d_node, node_saved, cols, rows_of, scale, small, weights, d_edges, edge_saved, d_before):
    levels, rows = lax.axis_size("lvl"), lax.axis_size("row")
    h, width = d_node.shape
    count = d_edges.shape[0]
    group = count // rows
    vmem = pl.BlockSpec(memory_space=pltpu.VMEM)
    hbm = pl.BlockSpec(memory_space=pl.ANY)
    shape = jax.ShapeDtypeStruct
    ins = (d_node,) + node_saved + (cols, rows_of, scale) + small + (d_before, d_edges) + edge_saved + weights
    outs = (
        shape((h, width), F32),
        shape((count, width) if last_layer else (16, 128), BF16),
        shape((count, width), BF16),
        shape((7 * width, width), BF16),
        shape((64, width), F32),
    )
    others = max(levels - 1, 1)
    return pl.pallas_call(
        functools.partial(backward_kernel, layer, levels, rows, last_layer),
        out_shape=outs,
        in_specs=[vmem] * (len(ins) - 10) + [hbm] * 10,
        out_specs=(vmem, hbm, hbm, vmem, vmem),
        scratch_shapes=[
            pltpu.VMEM((rows * h * levels, width), BF16),
            pltpu.VMEM((Scatter.receives(levels, rows), h, width), BF16),
            pltpu.VMEM((5, count, width), BF16),
            pltpu.VMEM((h * levels, width), BF16),
            pltpu.VMEM((h, width), F32),
            pltpu.VMEM((h * levels, width), F32),
            pltpu.VMEM((2, 2, 2 * group, width), BF16),
        ]
        + [pltpu.VMEM(weight.shape[1:], BF16) for weight in weights]
        + [
            pltpu.SemaphoreType.DMA((9,)),
            pltpu.SemaphoreType.DMA((2, 2)),
            pltpu.SemaphoreType.DMA((Scatter.sends(levels, rows),)),
            pltpu.SemaphoreType.DMA((2 * Scatter.receives(levels, rows),)),
            pltpu.SemaphoreType.DMA((others,)),
            pltpu.SemaphoreType.DMA((others,)),
        ],
        compiler_params=pltpu.CompilerParams(collective_id=3 + layer, has_side_effects=True, vmem_limit_bytes=VMEM_BYTES),
        name=f"backward_{layer}",
    )(*ins)


def sum_kernel(levels, rows, h, *refs):
    count = len(refs) - 9
    terms = refs[:count]
    out, stage, inbox, total, scatter_send, scatter_recv, gather_send, gather_recv, load_sem = refs[count:]
    g = Grid(levels, rows)
    pairs = []
    at = 0
    for term in terms:
        pairs.append((term, stage.at[pl.ds(at, term.shape[0])]))
        at += term.shape[0]
    loads = load_all(pairs, load_sem)
    g.greet()
    for copy in loads:
        copy.wait()
    rs = Scatter(g, stage, inbox, h, scatter_send, scatter_recv)
    rs.run(ahead=2)
    rs.last(total)
    ag = Gather(g, out, h, gather_send, gather_recv)
    ag.slot(g.row, g.l)[...] = total[...].astype(BF16)
    ag.run()
    rs.finish()
    ag.finish()


def sum_pieces(terms, call):
    levels, rows = lax.axis_size("lvl"), lax.axis_size("row")
    width = terms[0].shape[1]
    count = sum(term.shape[0] for term in terms)
    h = count // (levels * rows)
    return pl.pallas_call(
        functools.partial(sum_kernel, levels, rows, h),
        out_shape=jax.ShapeDtypeStruct((count, width), BF16),
        in_specs=[pl.BlockSpec(memory_space=pl.ANY)] * len(terms),
        out_specs=pl.BlockSpec(memory_space=pltpu.VMEM),
        scratch_shapes=[
            pltpu.VMEM((count, width), BF16),
            pltpu.VMEM((Scatter.receives(levels, rows), h, width), BF16),
            pltpu.VMEM((h, width), F32),
            pltpu.SemaphoreType.DMA((Scatter.sends(levels, rows),)),
            pltpu.SemaphoreType.DMA((2 * Scatter.receives(levels, rows),)),
            pltpu.SemaphoreType.DMA((Gather.sends(levels, rows),)),
            pltpu.SemaphoreType.DMA((2 * rows * levels,)),
            pltpu.SemaphoreType.DMA((len(terms),)),
        ],
        compiler_params=pltpu.CompilerParams(collective_id=call, has_side_effects=True, vmem_limit_bytes=VMEM_BYTES),
        name=f"sum_{call}",
    )(*terms)


def widen_kernel(parts, sums, *outs):
    i = pl.program_id(0)
    part = lax.rem(i, sum(parts))
    first = 0
    for count, out in zip(parts, outs):

        def write(out=out):
            out[0] = sums[...].astype(F32)

        pl.when((part >= first) & (part < first + count))(write)
        first += count


def widen(sums, layers, parts):
    width = sums.shape[1]
    each = sum(parts)
    specs = []
    first = 0
    for count in parts:

        def index(i, first=first, count=count):
            return i // each, jnp.clip(lax.rem(i, each) - first, 0, count - 1), 0

        specs.append(pl.BlockSpec((1, width, width), index))
        first += count
    return pl.pallas_call(
        functools.partial(widen_kernel, parts),
        grid=(layers * each,),
        out_shape=tuple(jax.ShapeDtypeStruct((layers, count * width, width), F32) for count in parts),
        in_specs=[pl.BlockSpec((width, width), lambda i: (i, 0))],
        out_specs=tuple(specs),
        name="widen",
    )(sums)


def on_device(
    node_latent, edge_latent, senders, receivers, live_edges,
    edge_w1, edge_b1, edge_w2, edge_b2, edge_gain, edge_shift, node_w1, node_b1, node_w2, node_b2, node_gain, node_shift,
    node_cotangent, edge_cotangent,
):
    node_count, width = node_latent.shape
    edge_count = edge_latent.shape[0]
    layers = edge_w1.shape[0]
    row_total, level_total = lax.axis_size("row"), lax.axis_size("lvl")
    half = node_count // level_total
    mine = lambda array: lax.dynamic_slice_in_dim(array, lax.axis_index("lvl") * half, half)
    cols, rows_of, edges, d_edges, place = order_edges(node_count, senders, receivers, live_edges, edge_latent, edge_cotangent)
    node = mine(node_latent)
    update = jnp.zeros((16, 128), BF16)
    saved = []
    tallies = []
    weights = (edge_w1, edge_w2, node_w1, node_w2)
    for layer in range(layers):
        small = (edge_b1, edge_b2, edge_gain, edge_shift, node_b1, node_b2, node_gain, node_shift)
        sent, pre, normed, update, new_edges, scale, block, node, recv, npre, nnormed, nscale, tally = forward_layer(
            layer, node, edges, update, cols, rows_of, small, weights
        )
        saved.append(((block, recv, npre, nnormed, nscale), scale, (pre, normed, edges, sent)))
        tallies.append(tally)
        edges = new_edges
    d_node = mine(node_cotangent)
    d_change = jnp.zeros((16, 128), BF16)
    grads = [None] * layers
    sums = [None] * layers
    for layer in reversed(range(layers)):
        node_saved, scale, edge_saved = saved[layer]
        d_node, d_edges, d_change, grads[layer], sums[layer] = backward_layer(
            layer, layer == layers - 1, d_node, node_saved, cols, rows_of, scale, (edge_gain, node_gain), weights, d_edges, edge_saved, d_change
        )
    small = jnp.concatenate([jnp.sum(part.reshape(8, 8, width), axis=1) for part in sums])
    squares = jnp.stack([jnp.sum(tally.reshape(4, 8 * width), axis=1) for tally in tallies])
    squares = jnp.pad(squares.reshape(1, -1), ((0, 0), (0, width - squares.size)))
    devices = row_total * level_total
    used = layers * 7 * width + small.shape[0] + 1
    share = -(-used // (16 * devices)) * 16
    rest = [small.astype(BF16), squares.astype(BF16), jnp.zeros((share * devices - used, width), BF16)]
    flat = sum_pieces(grads + [jnp.concatenate(rest)], 5)
    big = widen(flat, layers, (3, 1, 2, 1))
    after = layers * 7 * width
    smalls = flat[after : after + 8 * layers].astype(F32).reshape(layers, 8, width)
    squares = flat[after + 8 * layers, : 4 * layers].astype(F32).reshape(layers, 4)
    edge_out, edge_grad = restore_edges(place, update, d_change, edge_latent, edge_cotangent)
    node_entries = float(node_count * row_total * width)
    edge_entries = float(edge_count * row_total * level_total * width)
    entries = jnp.array([node_entries, edge_entries, edge_entries, node_entries], F32)
    both = lax.all_gather(jnp.stack([node, d_node]), "lvl", axis=1, tiled=True)
    return (
        both[0],
        edge_out,
        both[1],
        edge_grad,
        big[0],
        smalls[:, 0],
        big[1],
        smalls[:, 1],
        smalls[:, 2],
        smalls[:, 3],
        big[2],
        smalls[:, 4],
        big[3],
        smalls[:, 5],
        smalls[:, 6],
        smalls[:, 7],
        jnp.sqrt(squares / entries[None, :]),
    )


def solution(mesh):
    rows, both, whole = P("row", None), P(("lvl", "row"), None), P()
    edge = P(("lvl", "row"))
    placed = (rows, both, edge, edge, edge) + (whole,) * 12 + (rows, both)
    outs = (rows, both, rows, both) + (whole,) * 13
    return jax.shard_map(on_device, mesh=mesh, in_specs=placed, out_specs=outs, check_vma=False)
```

time: 1080 us -> 468 us (0.43)
  waiting for transfers between devices: 443 us -> 0.02 us
  Pallas kernels: 0 us -> 435 us
  local copies, waits for them, and re-layouts: 208 us -> 11.1 us
  other arithmetic: 185 us -> 5.64 us
  blocking collectives: 131 us -> 0 us
  matrix products: 84.1 us -> 0 us
    pallas_call x0 -> x8, Pallas kernels: none -> 435 us  [the longest x2 141 us: backward_layer(): pl.pallas_call(functools.partial(backward_kernel, layer, levels, rows, la...]
    psum x4 -> x0, waiting for transfers between devices: 191 us -> none  [the longest x1 175 us: on_device(): lax.psum((edge_first, edge_first_b, edge_second, edge_second_b, edge_gain...]
    reduce_scatter x2 -> x0, waiting for transfers between devices: 169 us -> none  [on_device(): lax.psum_scatter(jax.ops.segment_sum(d_send, target, num_segments=row_cou...]
    psum x4 -> x0, blocking collectives: 131 us -> none  [the longest x2 60.5 us: on_device(): received = lax.psum(partials, 'lvl')]
    dot_general x26 -> x0, matrix products: 84.1 us -> none  [the longest x16 56.8 us: contract(): lax.dot_general(left, right, (((left_dim,), (right_dim,)), ((), ())), pre...]
    gather x12 -> x0, local copies, waits for them, and re-layouts: 83.2 us -> none  [the longest x4 32.5 us: pick_rows(): fetched = jnp.take(shard_rows, jnp.clip(senders, 0, row_count - 1), axis=0)]
    all_gather x2 -> x1, waiting for transfers between devices: 83.1 us -> 0.01 us  [on_device(): both = lax.all_gather(jnp.stack([node, d_node]), 'lvl', axis=1, tiled=True)]
    scatter-add x4 -> x0, other arithmetic: 82 us -> none  [the longest x2 46.8 us: on_device(): jax.ops.segment_sum(d_send, target, num_segments=row_count + 1)[:row_count]]
  transfers between devices with their start and end apart: 8 -> 1, of which waited for: 6 -> 0; matrix products, arithmetic and copies ran while one was open for 18% -> 2% of each run, Pallas kernels for 0% -> 30%
where the time goes in v1:
time: 468 us; the launch traced here: 467 us
  Pallas kernels  435 us (93%)
  between operations  14.8 us (3%)
  local copies, waits for them, and re-layouts  11.1 us (2%)
  other arithmetic  5.64 us (1%)
    pallas_call x2, Pallas kernels, backward_layer(): pl.pallas_call(functools.partial(backward_kernel, layer, levels, rows, la...  141 us
    pallas_call x2, Pallas kernels, forward_layer(): pl.pallas_call(functools.partial(forward_kernel, layer, levels, rows, fir...  125 us
    pallas_call x1, Pallas kernels, sum_pieces(): pl.pallas_call(functools.partial(sum_kernel, levels, rows, h), out_shape=...  107 us
    pallas_call x1, Pallas kernels, order_edges(): pl.pallas_call(functools.partial(order_kernel, row_total, node_count), ou...  29.9 us
    pallas_call x1, Pallas kernels, restore_edges(): pl.pallas_call(restore_kernel, grid=(count // size,), out_shape=(jax.Shap...  18.9 us
    pallas_call x1, Pallas kernels, widen(): pl.pallas_call(functools.partial(widen_kernel, parts), grid=(layers * eac...  13.6 us
  transfers between devices with their start and end apart: 1, of which 0 were waited for; matrix products, arithmetic and copies ran while one was open for 2% of the time, Pallas kernels for 30%

profile of v1, /device:TPU:0, one launch (start us, length us, event | category | flops | bytes accessed | tf_op | source)
XLA Modules:
  0.0 466.7 jit_solution(5210840434674946341)
XLA Ops:
  7.9 2.2 constant_dynamic-slice_fusion
  10.1 29.9 %order_edges.1 = (f32[2560,128]{1,0:T(8,128)}, f32[16,8,160]{2,1,0:T(8,128)}, bf16[2560,512]{1,0:T(8,128)(2,1)}, bf16[2560,512]{1,0:T(8,128)(2,1)}, s32[20,128]{1,0:T(8,128)}) custom-call(s32[20,128]{1,0:T(8,128)} %bitcast.49, s32[20,128]{1,0:T(8,128)} %bitcast.50, s32[1,1]{1,0:T(1,128)} %bitcast.46.live, f32[2560,512]{1,0:T(8,128)} %edges.3, f32[2560,512]{1,0:T(8,128)} %cot.3), custom_call_target="tpu_custom_call" | custom-call | tf_op jit(solution)/shard_map/order_edges/pallas_call | solution.py:631
  40.0 0.6 broadcast_1_before_d_before.2.before.d_before
  40.6 63.2 %forward_0.1 = (bf16[2560,512]{1,0:T(8,128)(2,1)}, bf16[2560,512]{1,0:T(8,128)(2,1)}, bf16[2560,512]{1,0:T(8,128)(2,1)}, bf16[2560,512]{1,0:T(8,128)(2,1)}, bf16...) custom-call(f32[256,512]{1,0:T(8,128)} %get-tuple-element.118.node, ...), custom_call_target="tpu_custom_call" | custom-call | tf_op jit(solution)/shard_map/forward_0/pallas_call | solution.py:833
  103.9 61.9 %forward_1.1 = (bf16[2560,512]{1,0:T(8,128)(2,1)}, bf16[2560,512]{1,0:T(8,128)(2,1)}, bf16[2560,512]{1,0:T(8,128)(2,1)}, bf16[2560,512]{1,0:T(8,128)(2,1)}, bf16...) custom-call(f32[256,512]{1,0:T(8,128)} %get-tuple-element.65.node, ...), custom_call_target="tpu_custom_call" | custom-call | tf_op jit(solution)/shard_map/forward_1/pallas_call | solution.py:833
  165.8 68.5 %backward_1.1 = (f32[256,512]{1,0:T(8,128)}, bf16[2560,512]{1,0:T(8,128)(2,1)}, bf16[2560,512]{1,0:T(8,128)(2,1)}, bf16[3584,512]{1,0:T(8,128)(2,1)}, f32[64,512]{1,0:T(8,128)}) custom-call(f32[256,512]{1,0:T(8,128)} %get-tuple-element.117.d_node, bf16[512,512]{1,0:T(8,128)(2,1)} %get-tuple-element.69.block, bf16[256,512]{1,0:T(8,128)(2,1)} %get-tuple-element.70.recv, ...), custom_call_target="tpu_custom_call" | custom-call | tf_op jit(solution)/shard_map/backward_1/pallas_call | solution.py:1007
  234.3 72.3 %backward_0.1 = (f32[256,512]{1,0:T(8,128)}, bf16[16,128]{1,0:T(8,128)(2,1)}, bf16[2560,512]{1,0:T(8,128)(2,1)}, bf16[3584,512]{1,0:T(8,128)(2,1)}, f32[64,512]{1,0:T(8,128)}) custom-call(f32[256,512]{1,0:T(8,128)} %get-tuple-element.79.d_node, bf16[512,512]{1,0:T(8,128)(2,1)} %get-tuple-element.80.block, bf16[256,512]{1,0:T(8,128)(2,1)} %get-tuple-element.81.recv, ...), custom_call_target="tpu_custom_call" | custom-call | tf_op jit(solution)/shard_map/backward_0/pallas_call | solution.py:1007
  306.7 2.2 pad_maximum_fusion
  308.8 0.1 reduce_sum.55
  309.0 0.1 reduce_sum.56
  309.0 0.1 reduce_sum.57
  309.2 0.1 reduce_sum.52
  309.3 0.1 reduce_sum.53
  309.4 0.1 reduce_sum.54
  309.5 0.1 reshape.73
  309.8 0.9 fusion.3.refs_2_
  310.7 106.8 %sum_5.1.sums = bf16[7680,512]{1,0:T(8,128)(2,1)} custom-call(bf16[3584,512]{1,0:T(8,128)(2,1)} %get-tuple-element.97.refs_0_, bf16[3584,512]{1,0:T(8,128)(2,1)} %get-tuple-element.98.refs_1_, bf16[512,512]{1,0:T(8,128)(2,1)} %fusion.3.refs_2_), custom_call_target="tpu_custom_call" | custom-call | tf_op jit(solution)/shard_map/sum_5/pallas_call | solution.py:1064
  417.5 13.6 %widen.1 = (f32[2,1536,512]{2,1,0:T(8,128)}, f32[2,512,512]{2,1,0:T(8,128)}, f32[2,1024,512]{2,1,0:T(8,128)}, f32[2,512,512]{2,1,0:T(8,128)}) custom-call(bf16[7680,512]{1,0:T(8,128)(2,1)} %sum_5.1.sums), custom_call_target="tpu_custom_call" | custom-call | tf_op jit(solution)/shard_map/widen/pallas_call | solution.py:1109
  431.1 0.7 bitcast_convert_fusion
  431.8 0.6 copy.61
  432.4 0.6 copy.62
  433.0 0.6 copy.63
  433.6 0.6 copy.64
  434.2 0.6 copy.65
  434.8 0.6 copy.66
  435.4 0.6 copy.67
  436.0 0.6 copy.68
  436.6 0.7 convert_reduce_fusion
  437.3 0.1 reshape.78
  437.4 18.9 %restore_edges.1 = (f32[2560,512]{1,0:T(8,128)}, f32[2560,512]{1,0:T(8,128)}) custom-call(s32[20,128]{1,0:T(8,128)} %get-tuple-element.92.place, bf16[2560,512]{1,0:T(8,128)(2,1)} %get-tuple-element.93.update, bf16[2560,512]{1,0:T(8,128)(2,1)} %get-tuple-element.94.d_edge, f32[2560,512]{1,0:T(8,128)} %edges.3, f32[2560,512]{1,0:T(8,128)} %cot.3), custom_call_target="tpu_custom_call" | custom-call | tf_op jit(solution)/shard_map/restore_edges/pallas_call | solution.py:667
  456.3 0.6 multiply_sqrt_fusion
  456.8 3.0 slice_bitcast_fusion
  (21 shorter events, 0.3 us)
Async XLA Ops:
  7.2 449.7 %all-gather.2.cloned.1.call-start = ((), (), s32[]{:S(2)}) async-start(), calls=%async_computation | async-start | bytes 3145728 | tf_op jit(solution)/shard_map/all_gather | solution.py:1169
  234.3 72.3 %copy-start = (f32[256,512]{1,0:T(8,128)S(1)}, f32[256,512]{1,0:T(8,128)}, u32[]{:S(2)}) copy-start(f32[256,512]{1,0:T(8,128)} %get-tuple-element.68) | copy-start | bytes 1572868
  306.6 2.2 copy-start.4
  306.6 2.6 copy-start.3
  306.6 3.1 copy-start.2
  306.6 3.1 copy-start.1
  437.4 18.9 %copy-start.5 = (f32[4]{0:T(128)S(1)}, f32[4]{0:T(128)}, u32[]{:S(2)}) copy-start(f32[4]{0:T(128)} %constant.25) | copy-start | bytes 52
Sparse Core Ops, SparseCore 0:
  308.9 45.6 all-gather.1
